TPU v7x, 128 devices: a whole 4x4x4 slice. The times are simulated.
128 devices in a mesh: expert: 32 (over y, x, z_lo), slab: 4 (over z_hi, core).
Axes of the slice: x: 4, y: 4, z: 4 (z_hi: 2, z_lo: 2; z = z_hi * 2 + z_lo), core: 2. Of those that a mesh axis runs over, the one named last changes fastest.
Arguments:
- tokens: bfloat16 [8192, 4096], P('expert', 'slab'), may hold values from -45 to 45
- grad_out: bfloat16 [8192, 4096], P('expert', 'slab'), may hold values from -3 to 3
- position: int32 [8192], P('expert'), may hold values from 0 to 8191, as said below
- centroid: bfloat16 [32, 4096], P('expert'), may hold values from -0.09375 to 0.09375
- gain: bfloat16 [32, 4096], P('expert'), may hold values from 0.099609375 to 1.8984375
- w_in: bfloat16 [32, 4096, 4096], P('expert', None, 'slab'), may hold values from -0.09375 to 0.09375
- w_out: bfloat16 [32, 4096, 4096], P('expert', 'slab'), may hold values from -0.09375 to 0.09375
Outputs:
- input_grad: bfloat16 [8192, 4096], P('expert', 'slab')
- centroid_grad: float32 [32, 4096], P('expert', 'slab')
Inputs may be any that keep to these rules, and one draw needn't show every extreme that they name: position is a permutation of the token numbers, so every expert gets exactly 256 tokens; the 256 tokens of one index of expert go at most 12 to one expert, and in every draw some index sends exactly 12 to some expert.
All inputs are finite; a program needn't handle non-finite values.
Results may differ from a plain program's by a relative error of at most 0.015.
Values may be sent and summed in bfloat16 or wider, within the bound.
A program may use at most 128 MiB of HBM per device.

v0:
```python
import math

import jax
import jax.numpy as jnp
from jax import lax
from jax.sharding import PartitionSpec as P

gelu_root = math.sqrt(2.0 / math.pi)


def gelu_pair(pre):
    tangent = jnp.tanh(gelu_root * (pre + 0.044715 * pre * pre * pre))
    value = 0.5 * pre * (1.0 + tangent)
    slope = 0.5 * (1.0 + tangent) + 0.5 * pre * (1.0 - tangent * tangent) * gelu_root * (
        1.0 + 3.0 * 0.044715 * pre * pre
    )
    return (value, slope)


def per_device(tokens, grad_out, position, centroid, gain, w_in, w_out):
    expert_count = lax.axis_size("expert")
    tok_rows = tokens.shape[0]
    slice_width = tokens.shape[1]
    full_width = centroid.shape[1]
    capacity = tok_rows // expert_count + tok_rows // (2 * expert_count)
    slots = expert_count * capacity
    target = position // tok_rows
    onehot = (target[:, None] == jnp.arange(expert_count, dtype=jnp.int32)[None, :]).astype(
        jnp.int32
    )
    earlier = jnp.cumsum(onehot, axis=0) - onehot
    rank_in = jnp.sum(earlier * onehot, axis=1)
    slot_of = target * capacity + rank_in
    source = jnp.zeros((slots,), jnp.int32).at[slot_of].set(jnp.arange(tok_rows, dtype=jnp.int32))
    filled = jnp.zeros((slots,), jnp.bool_).at[slot_of].set(True)

    def pack(rows):
        return jnp.where(filled[:, None], jnp.take(rows, source, axis=0), jnp.zeros((), rows.dtype))

    slab_index = lax.axis_index("slab")
    whole_x, whole_dy = (
        lax.all_gather(tokens, "slab", axis=1, tiled=True),
        lax.all_gather(grad_out, "slab", axis=1, tiled=True),
    )
    recv_x, recv_dy = (
        lax.all_to_all(pack(whole_x), "expert", split_axis=0, concat_axis=0, tiled=True),
        lax.all_to_all(pack(whole_dy), "expert", split_axis=0, concat_axis=0, tiled=True),
    )
    part_x = lax.dynamic_slice_in_dim(recv_x, slab_index * slice_width, slice_width, 1)
    center = centroid[0]
    gain_wide = gain[0].astype(jnp.float32)
    logit = jnp.dot(recv_x, center, preferred_element_type=jnp.float32)
    gate = jax.nn.sigmoid(logit)
    wide_x = recv_x.astype(jnp.float32)
    row_mean = jnp.mean(wide_x, axis=1)
    centered = wide_x - row_mean[:, None]
    variance = jnp.mean(centered * centered, axis=1)
    inv_scale = lax.rsqrt(variance + 1e-05)
    normed = (centered * inv_scale[:, None] * gain_wide[None, :]).astype(jnp.bfloat16)
    pre = jnp.dot(normed, w_in[0], preferred_element_type=jnp.float32)
    active, slope = gelu_pair(pre)
    back = lax.dot_general(
        recv_dy, w_out[0], (((1,), (1,)), ((), ())), preferred_element_type=jnp.float32
    )
    gate_part = jnp.sum(active * back, axis=1)
    delta = (gate[:, None] * back * slope).astype(jnp.bfloat16)
    weight_rows = w_in[0]
    grad_normed = lax.psum_scatter(
        lax.dot_general(
            weight_rows, delta, (((1,), (1,)), ((), ())), preferred_element_type=jnp.float32
        ).astype(jnp.bfloat16),
        "slab",
        scatter_dimension=0,
        tiled=True,
    ).astype(jnp.float32)
    part_wide = part_x.astype(jnp.float32).T
    part_hat = (part_wide - row_mean[None, :]) * inv_scale[None, :]
    gain_part = lax.dynamic_slice_in_dim(gain_wide, slab_index * slice_width, slice_width, 0)
    scaled = grad_normed * gain_part[:, None]
    gate_total, first_sum, second_sum = lax.psum(
        (gate_part, jnp.sum(scaled, axis=0), jnp.sum(scaled * part_hat, axis=0)), "slab"
    )
    mean_one = first_sum / full_width
    mean_two = second_sum / full_width
    gate_grad = gate_total * gate * (1.0 - gate)
    center_part = lax.dynamic_slice_in_dim(center, slab_index * slice_width, slice_width, 0).astype(
        jnp.float32
    )
    grad_rows = inv_scale[None, :] * (scaled - mean_one[None, :] - part_hat * mean_two[None, :])
    grad_rows = (grad_rows + gate_grad[None, :] * center_part[:, None]).astype(jnp.bfloat16)
    centroid_grad = jnp.sum(part_wide * gate_grad[None, :], axis=1)[None, :]
    returned = lax.all_to_all(grad_rows, "expert", split_axis=1, concat_axis=1, tiled=True)
    input_grad = jnp.take(returned, slot_of, axis=1).T
    return (input_grad, centroid_grad)


def solution(mesh):
    placed = (
        P("expert", "slab"),
        P("expert", "slab"),
        P("expert"),
        P("expert", None),
        P("expert", None),
        P("expert", None, "slab"),
        P("expert", "slab", None),
    )
    return jax.shard_map(
        per_device,
        mesh=mesh,
        in_specs=placed,
        out_specs=(P("expert", "slab"), P("expert", "slab")),
        check_vma=False,
    )
```

profile of v0, /device:TPU:1, one launch (start us, length us, event | category | flops | bytes accessed | tf_op | source)
XLA Modules:
  0.0 334.3 jit_solution(13767775477776406656)
XLA Ops:
  14.6 25.5 %all-gather.3.cloned.1.call-done = bf16[256,4096]{1,0:T(8,128)(2,1)} async-done(((bf16[256,1024]{1,0:T(8,128)(2,1)}), bf16[256,4096]{1,0:T(8,128)(2,1)}) %all-gather.3.cloned.1.call-update) | async-done | bytes 2097168 | tf_op jit(solution)/shard_map/all_gather | solution.py:42
  40.1 10.1 %gather_fusion.1 = bf16[384,4096]{1,0:T(8,128)(2,1)} fusion(bf16[256,4096]{1,0:T(8,128)(2,1)} %all-gather.3.cloned.1.call-done, s32[1024]{0:T(1024)S(1)} %pad_clamp_fusion.1), kind=kCustom, calls=%fused_computation.clone | custom fusion | bytes 6292992 | tf_op jit(solution)/shard_map/jit(_take)/gather | solution.py:38
  50.2 17.6 %all-gather.5.cloned.1.call-done = bf16[256,4096]{1,0:T(8,128)(2,1)} async-done(((bf16[256,1024]{1,0:T(8,128)(2,1)}), bf16[256,4096]{1,0:T(8,128)(2,1)}) %all-gather.5.cloned.1.call-update) | async-done | bytes 2097168 | tf_op jit(solution)/shard_map/all_gather | solution.py:43
  67.8 10.1 %gather_fusion.2 = bf16[384,4096]{1,0:T(8,128)(2,1)} fusion(bf16[256,4096]{1,0:T(8,128)(2,1)} %all-gather.5.cloned.1.call-done, s32[1024]{0:T(1024)S(1)} %pad_clamp_fusion.1), kind=kCustom, calls=%fused_computation.1.clone | custom fusion | bytes 6292992 | tf_op jit(solution)/shard_map/jit(_take)/gather | solution.py:38
  77.9 4.5 %select_select_fusion = (bf16[384,4096]{1,0:T(8,128)(2,1)S(1)}, bf16[384,4096]{1,0:T(8,128)(2,1)}) fusion(bf16[384,4096]{1,0:T(8,128)(2,1)} %gather_fusion.2, pred[384]{0:T(512)(128)(4,1)S(1)} %compare_and_fusion, pred[384]{0:T(512)(128)(4,1)S(1)} %scatter_custom_fusion, bf16[384,4096]{1,0:T(8,128)(2,1)} %gather_fusion.1), kind=kLoop, calls=%fused_computation.20 | loop fusion | flops 6291456 | bytes 12583680 | tf_op jit(solution)/shard_map/jit(_where)/select_n | solution.py:38
  82.4 5.5 %all_to_all.24 = bf16[32,12,4096]{2,1,0:T(8,128)(2,1)} reshape(bf16[384,4096]{1,0:T(8,128)(2,1)} %get-tuple-element.11) | data formatting | bytes 6291456 | tf_op jit(solution)/shard_map/all_to_all | solution.py:46
  87.9 7.2 %all-to-all-start = ((bf16[32,12,4096]{2,1,0:T(8,128)(2,1)}), bf16[32,12,4096]{2,1,0:T(8,128)(2,1)}, u32[]{:S(2)}, u32[]{:S(2)}) async-start(bf16[32,12,4096]{2,1,0:T(8,128)(2,1)} %all_to_all.24), calls=%async_computation | async-start | bytes 8388608 | tf_op jit(solution)/shard_map/all_to_all | solution.py:46
  97.8 57.6 %all-to-all-done = bf16[32,12,4096]{2,1,0:T(8,128)(2,1)} async-done(((bf16[32,12,4096]{2,1,0:T(8,128)(2,1)}), bf16[32,12,4096]{2,1,0:T(8,128)(2,1)}, u32[]{:S(2)}, u32[]{:S(2)}) %all-to-all-start) | async-done | bytes 3145760 | tf_op jit(solution)/shard_map/all_to_all | solution.py:46
  155.4 6.3 %all-to-all-start.1 = ((bf16[32,12,4096]{2,1,0:T(8,128)(2,1)}), bf16[32,12,4096]{2,1,0:T(8,128)(2,1)}, u32[]{:S(2)}, u32[]{:S(2)}) async-start(bf16[32,12,4096]{2,1,0:T(8,128)(2,1)} %all_to_all.27), calls=%async_computation.1 | async-start | bytes 8388608 | tf_op jit(solution)/shard_map/all_to_all | solution.py:47
  161.7 2.9 convert_reduce_fusion
  164.6 3.6 %fusion.2 = f32[32,12]{1,0:T(8,128)S(1)} fusion(bf16[32,12,4096]{2,1,0:T(8,128)(2,1)} %all-to-all-done, f32[32,12]{1,0:T(8,128)S(1)} %broadcast_multiply_fusion), kind=kLoop, calls=%fused_computation.9 | loop fusion | flops 6291072 | bytes 3148800 | tf_op jit(solution)/shard_map/reduce_sum | solution.py:57
  168.2 6.4 %fusion.4 = bf16[32,12,4096]{2,1,0:T(8,128)(2,1)} fusion(bf16[32,12,4096]{2,1,0:T(8,128)(2,1)} %all-to-all-done, f32[4096]{0:T(1024)S(1)} %bitcast.67, f32[32,12]{1,0:T(8,128)S(1)} %add_rsqrt_fusion, f32[32,12]{1,0:T(8,128)S(1)} %broadcast_multiply_fusion), kind=kLoop, calls=%fused_computation.11 | loop fusion | flops 7864320 | bytes 6310912 | tf_op jit(solution)/shard_map/convert_element_type | solution.py:59
  174.7 5.6 %convert_element_type.56 = bf16[384,4096]{1,0:T(8,128)(2,1)} reshape(bf16[32,12,4096]{2,1,0:T(8,128)(2,1)} %fusion.4) | data formatting | bytes 6291456 | tf_op jit(solution)/shard_map/convert_element_type | solution.py:59
  180.3 4.0 %all_to_all.26 = bf16[384,4096]{1,0:T(8,128)(2,1)S(1)} reshape(bf16[32,12,4096]{2,1,0:T(8,128)(2,1)} %all-to-all-done) | data formatting | bytes 6291456 | tf_op jit(solution)/shard_map/all_to_all | solution.py:46
  186.1 7.0 %fusion.7 = f32[384,1024]{1,0:T(8,128)} fusion(bf16[384,4096]{1,0:T(8,128)(2,1)S(1)} %copy-done, bf16[1,4096,1024]{2,1,0:T(8,128)(2,1)} %param.14), kind=kOutput, calls=%fused_computation.14 | convolution fusion | flops 3221225472 | bytes 13107200 | tf_op jit(solution)/shard_map/dot_general | solution.py:60
  193.2 25.3 %all-to-all-done.1 = bf16[32,12,4096]{2,1,0:T(8,128)(2,1)} async-done(((bf16[32,12,4096]{2,1,0:T(8,128)(2,1)}), bf16[32,12,4096]{2,1,0:T(8,128)(2,1)}, u32[]{:S(2)}, u32[]{:S(2)}) %all-to-all-start.1) | async-done | bytes 3145760 | tf_op jit(solution)/shard_map/all_to_all | solution.py:47
  218.5 5.6 %all_to_all.29 = bf16[384,4096]{1,0:T(8,128)(2,1)} reshape(bf16[32,12,4096]{2,1,0:T(8,128)(2,1)} %all-to-all-done.1) | data formatting | bytes 6291456 | tf_op jit(solution)/shard_map/all_to_all | solution.py:47
  224.1 8.6 %multiply_reduce_fusion = (f32[384]{0:T(512)S(1)}, f32[384,1024]{1,0:T(8,128)S(1)}) fusion(f32[384,1024]{1,0:T(8,128)} %fusion.7, bf16[384,4096]{1,0:T(8,128)(2,1)} %all_to_all.29, bf16[1,1024,4096]{2,1,0:T(8,128)(2,1)} %param.15), kind=kOutput, calls=%fused_computation.43 | convolution fusion | flops 3225157120 | bytes 14681600 | tf_op jit(solution)/shard_map/dot_general | solution.py:62
  232.7 11.2 %fusion.14 = bf16[4096,384]{0,1:T(8,128)(2,1)} fusion(bf16[1,4096,1024]{2,1,0:T(8,128)(2,1)} %param.14, f32[384,1024]{1,0:T(8,128)S(1)} %copy-done.3, f32[384,1024]{1,0:T(8,128)S(1)} %get-tuple-element.13, f32[384]{0:T(512)S(1)} %add_divide_fusion), kind=kOutput, calls=%fused_computation.19 | convolution fusion | flops 3230662656 | bytes 14681600 | tf_op jit(solution)/shard_map/dot_general | solution.py:69
  244.2 43.3 %reduce-scatter.2.cloned.1.call-done = bf16[1024,384]{0,1:T(8,128)(2,1)} async-done(((bf16[4096,384]{0,1:T(8,128)(2,1)}), bf16[1024,384]{0,1:T(8,128)(2,1)}) %reduce-scatter.2.cloned.1.call-update) | async-done | bytes 786448 | tf_op jit(solution)/shard_map/reduce_scatter | solution.py:68
  289.2 7.3 %all-reduce = (f32[384]{0:T(512)S(1)}, f32[384]{0:T(512)S(1)}, f32[384]{0:T(512)S(1)}) all-reduce(f32[384]{0:T(512)S(1)} %get-tuple-element.12, f32[384]{0:T(512)S(1)} %get-tuple-element.4, f32[384]{0:T(512)S(1)} %get-tuple-element.3), channel_id=1, replica_groups=mesh['expert'=32,'slab'=4] {'slab'}, use_global_device_ids=true, to_apply=%region_13.15 | all-reduce | flops 1152 | bytes 9216 | tf_op jit(solution)/shard_map/psum | solution.py:80
  296.5 2.7 fusion.25
  301.4 7.0 %all-to-all-start.2 = ((bf16[1024,32,12]{0,2,1:T(8,128)(2,1)}), bf16[1024,32,12]{0,2,1:T(8,128)(2,1)}, u32[]{:S(2)}, u32[]{:S(2)}) async-start(bf16[1024,32,12]{0,2,1:T(8,128)(2,1)} %all_to_all.30), calls=%async_computation.3 | async-start | bytes 2097152 | tf_op jit(solution)/shard_map/all_to_all | solution.py:92
  309.2 15.1 %all-to-all-done.2 = bf16[1024,32,12]{0,2,1:T(8,128)(2,1)} async-done(((bf16[1024,32,12]{0,2,1:T(8,128)(2,1)}), bf16[1024,32,12]{0,2,1:T(8,128)(2,1)}, u32[]{:S(2)}, u32[]{:S(2)}) %all-to-all-start.2) | async-done | bytes 786464 | tf_op jit(solution)/shard_map/all_to_all | solution.py:92
  (49 shorter events, 20.3 us)
Async XLA Ops:
  7.2 32.9 %all-gather.3.cloned.1.call-start = ((), (), s32[]{:S(2)}) async-start(), calls=%async_computation.4 | async-start | bytes 2621440 | tf_op jit(solution)/shard_map/all_gather | solution.py:42
  7.9 59.9 %all-gather.5.cloned.1.call-start = ((), (), s32[]{:S(2)}) async-start(), calls=%async_computation.5 | async-start | bytes 2621440 | tf_op jit(solution)/shard_map/all_gather | solution.py:43
  87.9 7.2 %copy-start.2 = (bf16[1,4096]{1,0:T(2,128)(2,1)S(1)}, bf16[1,4096]{1,0:T(2,128)(2,1)}, u32[]{:S(2)}) copy-start(bf16[1,4096]{1,0:T(2,128)(2,1)} %param.13) | copy-start | bytes 24580
  87.9 67.5 %all-to-all-start = ((bf16[32,12,4096]{2,1,0:T(8,128)(2,1)}), bf16[32,12,4096]{2,1,0:T(8,128)(2,1)}, u32[]{:S(2)}, u32[]{:S(2)}) async-start(bf16[32,12,4096]{2,1,0:T(8,128)(2,1)} %all_to_all.24), calls=%async_computation | async-start | bytes 8388608 | tf_op jit(solution)/shard_map/all_to_all | solution.py:46
  155.4 63.1 %all-to-all-start.1 = ((bf16[32,12,4096]{2,1,0:T(8,128)(2,1)}), bf16[32,12,4096]{2,1,0:T(8,128)(2,1)}, u32[]{:S(2)}, u32[]{:S(2)}) async-start(bf16[32,12,4096]{2,1,0:T(8,128)(2,1)} %all_to_all.27), calls=%async_computation.1 | async-start | bytes 8388608 | tf_op jit(solution)/shard_map/all_to_all | solution.py:47
  161.6 125.9 %reduce-scatter.2.cloned.1.call-start = ((), (), s32[]{:S(2)}) async-start(), calls=%async_computation.6 | async-start | bytes 3932160 | tf_op jit(solution)/shard_map/reduce_scatter | solution.py:68
  180.3 4.0 %copy-start.1 = (bf16[1,4096]{1,0:T(2,128)(2,1)S(1)}, bf16[1,4096]{1,0:T(2,128)(2,1)}, u32[]{:S(2)}) copy-start(bf16[1,4096]{1,0:T(2,128)(2,1)} %param.12) | copy-start | bytes 24580
  184.3 1.9 copy-start
  224.1 8.6 %copy-start.3 = (f32[384,1024]{1,0:T(8,128)S(1)}, f32[384,1024]{1,0:T(8,128)}, u32[]{:S(2)}) copy-start(f32[384,1024]{1,0:T(8,128)} %fusion.7) | copy-start | bytes 4718596
  301.4 22.9 %all-to-all-start.2 = ((bf16[1024,32,12]{0,2,1:T(8,128)(2,1)}), bf16[1024,32,12]{0,2,1:T(8,128)(2,1)}, u32[]{:S(2)}, u32[]{:S(2)}) async-start(bf16[1024,32,12]{0,2,1:T(8,128)(2,1)} %all_to_all.30), calls=%async_computation.3 | async-start | bytes 2097152 | tf_op jit(solution)/shard_map/all_to_all | solution.py:92
Sparse Core Ops, SparseCore 0:
  9.7 30.3 all-gather.2
  41.8 25.9 all-gather.4
  244.1 43.4 reduce-scatter.1
where the time goes:
time: 337 us; the launch traced here: 334 us
  waiting for transfers between devices  186 us (55%)
  local copies, waits for them, and re-layouts  52.5 us (16%)
  matrix products  27.7 us (8%)
  other arithmetic  26.5 us (8%)
  starting transfers between devices  20.6 us (6%)
  between operations  14 us (4%)
  blocking collectives  7.27 us (2%)
    all_to_all x1, waiting for transfers between devices, per_device(): lax.all_to_all(pack(whole_x), 'expert', split_axis=0, concat_axis=0, tile...  57.6 us
    reduce_scatter x1, waiting for transfers between devices, per_device(): lax.psum_scatter(lax.dot_general(weight_rows, delta, (((1,), (1,)), ((),...  43.3 us
    all_gather x1, waiting for transfers between devices, per_device(): lax.all_gather(tokens, 'slab', axis=1, tiled=True)  25.5 us
    all_to_all x1, waiting for transfers between devices, per_device(): lax.all_to_all(pack(whole_dy), 'expert', split_axis=0, concat_axis=0, til...  25.3 us
    gather x2, local copies, waits for them, and re-layouts, pack(): jnp.take(rows, source, axis=0)  20.2 us
    all_gather x1, waiting for transfers between devices, per_device(): lax.all_gather(grad_out, 'slab', axis=1, tiled=True)  17.6 us
    all_to_all x1, waiting for transfers between devices, per_device(): lax.all_to_all(grad_rows, 'expert', split_axis=1, concat_axis=1, tiled=True)  15.1 us
    dot_general x1, matrix products, per_device(): lax.dot_general(weight_rows, delta, (((1,), (1,)), ((), ())), preferred_e...  11.2 us
  transfers between devices with their start and end apart: 6, of which 6 were waited for; matrix products, arithmetic and copies ran while one was open for 13% of the time, Pallas kernels for 0%

commit v1 on v0

v1 whole, which is shorter than its diff:
```python
import functools
import math

import jax
import jax.numpy as jnp
from jax import lax
from jax.experimental import pallas as pl
from jax.experimental.pallas import tpu as pltpu
from jax.sharding import PartitionSpec as P

F32 = jnp.float32
BF16 = jnp.bfloat16
MESH = pl.DeviceIdType.MESH
ROWS = 16
ROOT = math.sqrt(2.0 / math.pi)
N_SLAB = 4


def iota(shape, dim):
    return lax.broadcasted_iota(jnp.int32, shape, dim)


def onehot(mask):
    return jnp.where(mask, 1.0, 0.0).astype(BF16)


def dot(a, b):
    return jnp.dot(a, b, preferred_element_type=F32)


def dot_t(a, b):
    return lax.dot_general(a, b, (((1,), (1,)), ((), ())), preferred_element_type=F32)


def kernel(
    n_exp,
    pos_ref,
    cent_ref,
    gain_ref,
    tok_hbm,
    dy_hbm,
    win_hbm,
    wout_hbm,
    out_ref,
    cgrad_ref,
    tok,
    gdy,
    win,
    wout,
    pick,
    pick_t,
    px,
    pd,
    rx,
    rd,
    comp,
    comp_t,
    xf,
    df,
    nx,
    pre,
    act,
    slp,
    bk,
    delta,
    usum,
    cols,
    stat,
    part_send,
    part_recv,
    far_acc,
    far_send,
    far_recv,
    mine_send,
    mine_recv,
    own,
    yy,
    pg,
    rg,
    lsem,
    a2a_s,
    a2a_r,
    ag_s,
    ag_r,
    rs_s,
    rs_r,
    st_s,
    st_r,
):
    rows, width = tok.shape
    full = N_SLAB * width
    ff = win.shape[1]
    quarter = width // 4
    slots = n_exp * ROWS
    me = lax.axis_index("expert")
    slab = lax.axis_index("slab")
    hi, core = slab // 2, slab % 2
    partner = hi * 2 + (1 - core)
    far = (1 - hi) * 2 + core
    far_partner = (1 - hi) * 2 + (1 - core)

    cp_tok = pltpu.make_async_copy(tok_hbm, tok, lsem.at[0])
    cp_dy = pltpu.make_async_copy(dy_hbm, gdy, lsem.at[1])
    cp_win = pltpu.make_async_copy(win_hbm, win, lsem.at[2])
    cp_wout = pltpu.make_async_copy(wout_hbm, wout, lsem.at[3])
    cp_tok.start()
    cp_dy.start()

    bar = pltpu.get_barrier_semaphore()

    @pl.loop(1, n_exp)
    def _(k):
        pl.semaphore_signal(
            bar, inc=1, device_id={"expert": lax.rem(me + k, n_exp)}, device_id_type=MESH
        )

    for peer in (partner, far, far_partner):
        pl.semaphore_signal(bar, inc=1, device_id={"slab": peer}, device_id_type=MESH)
    cp_win.start()
    cp_wout.start()

    pos = pos_ref[...]
    tgt = lax.div(pos, rows)
    row = pos - tgt * rows
    hit = iota((n_exp, rows), 0) == tgt
    before = dot(onehot(hit), onehot(iota((rows, rows), 0) < iota((rows, rows), 1)))
    rank = jnp.sum(jnp.where(hit, before, 0.0), axis=0, keepdims=True).astype(jnp.int32)
    third = lax.shift_right_logical(rank * 11, 5)
    rem3 = rank - 3 * third
    slot = [tgt * ROWS + rank]
    for j in range(3):
        slot.append(jnp.where(rem3 == j, tgt * ROWS + 12 + third, -1))
    for k in range(4):
        pick[k] = onehot(iota((slots, rows), 0) == slot[k])

    row_one = jnp.broadcast_to((row + 1).astype(F32), (128, rows))
    meta = None
    for k in range(4):
        marks = jnp.where(iota((128, rows), 0) // 32 == k, row_one, 0.0).astype(BF16)
        term = dot_t(pick[k], marks)
        meta = term if meta is None else meta + term
    px[:, pl.ds(3 * quarter, 128)] = meta.astype(BF16)

    def pack(into, take, source):
        for j in range(3):
            cols_j = pl.ds(j * quarter, quarter)
            value = dot(take[0], source[:, cols_j]) + dot(
                take[1 + j], source[:, pl.ds(3 * quarter, quarter)]
            )
            into[:, cols_j] = value.astype(BF16)

    mine = pl.ds(pl.multiple_of(me * ROWS, ROWS), ROWS)

    def send_all(source, target, idx):
        @pl.loop(1, n_exp)
        def _(k):
            d = lax.rem(me + k, n_exp)
            pltpu.make_async_remote_copy(
                src_ref=source.at[pl.ds(pl.multiple_of(d * ROWS, ROWS), ROWS)],
                dst_ref=target.at[mine],
                send_sem=a2a_s.at[idx],
                recv_sem=a2a_r.at[idx],
                device_id={"expert": d},
                device_id_type=MESH,
            ).start()

    def wait_bytes(ref, sem):
        part = ref.at[pl.ds(0, (n_exp - 1) * ROWS)]
        pltpu.make_async_copy(part, part, sem).wait()

    cp_tok.wait()
    pack(px, pick, tok)
    rx[mine, :] = px[mine, :]
    pl.semaphore_wait(bar, n_exp - 1 + 3)
    send_all(px, rx, 0)
    cp_dy.wait()
    pack(pd, pick, gdy)
    rd[mine, :] = pd[mine, :]
    send_all(pd, rd, 1)

    turned = [
        jnp.transpose(jnp.broadcast_to(slot[k].astype(F32), (128, rows)))[:, 0:1] for k in range(4)
    ]
    for k in range(4):
        pick_t[k] = onehot(iota((rows, slots), 1).astype(F32) == turned[k])
    cp_win.wait()
    gain_rows = jnp.broadcast_to(gain_ref[...], (16, full))

    @pl.loop(0, ff // 256)
    def _(n):
        cs = pl.ds(pl.multiple_of(n * 256, 256), 256)
        usum[:, cs] = dot(gain_rows, win[:, cs])[0:8]

    def gather_copy(buf, which, tile, source, kind, to):
        cs = pl.ds(tile * quarter, quarter)
        idx = (which * 3 + kind) * 4 + tile
        return pltpu.make_async_remote_copy(
            src_ref=buf.at[source, :, cs],
            dst_ref=buf.at[source, :, cs],
            send_sem=ag_s.at[idx],
            recv_sem=ag_r.at[idx],
            device_id={"slab": to},
            device_id_type=MESH,
        )

    def dense(recv, buf, which):
        for tile in range(4):
            cs = pl.ds(tile * quarter, quarter)
            if tile < 3:
                value = dot(comp[0], recv[:, cs])
            else:
                value = dot(comp[1], recv[:, pl.ds(0, quarter)])
                value += dot(comp[2], recv[:, pl.ds(quarter, quarter)])
                value += dot(comp[3], recv[:, pl.ds(2 * quarter, quarter)])
            buf[slab, :, cs] = value.astype(BF16)
            gather_copy(buf, which, tile, slab, 0, far).start()
            gather_copy(buf, which, tile, slab, 1, partner).start()

    def forward(buf, which, tile):
        gather_copy(buf, which, tile, far, 0, far).wait_recv()
        gather_copy(buf, which, tile, far, 2, partner).start()

    wait_bytes(rx, a2a_r.at[0])
    marks_in = rx[:, pl.ds(3 * quarter, 128)].astype(F32)
    marks_t = jnp.transpose(marks_in)
    for k in range(4):
        comp[k] = onehot((iota((rows, slots), 0) + 1).astype(F32) == marks_t[32 * k : 32 * k + 1])
    dense(rx, xf, 0)
    for k in range(4):
        comp_t[k] = onehot(
            (iota((slots, rows), 1) + 1).astype(F32) == marks_in[:, 32 * k : 32 * k + 1]
        )
    wait_bytes(rd, a2a_r.at[1])
    dense(rd, df, 1)

    for tile in range(4):
        forward(xf, 0, tile)
    for tile in range(4):
        gather_copy(xf, 0, tile, partner, 1, partner).wait_recv()
    for tile in range(4):
        gather_copy(xf, 0, tile, far_partner, 2, partner).wait_recv()

    step = 16

    @pl.loop(0, rows // step)
    def _(i):
        rs = pl.ds(pl.multiple_of(i * step, step), step)
        xs = [xf[b, rs, :].astype(F32) for b in range(N_SLAB)]
        total = None
        logit = None
        for b in range(N_SLAB):
            c_b = cent_ref[:, pl.ds(b * width, width)].astype(F32)
            t_b = jnp.sum(xs[b], axis=1, keepdims=True)
            l_b = jnp.sum(xs[b] * c_b, axis=1, keepdims=True)
            total = t_b if total is None else total + t_b
            logit = l_b if logit is None else logit + l_b
        mean = total * (1.0 / full)
        spread = None
        for b in range(N_SLAB):
            xs[b] = xs[b] - mean
            v_b = jnp.sum(xs[b] * xs[b], axis=1, keepdims=True)
            spread = v_b if spread is None else spread + v_b
        inv = lax.rsqrt(spread * (1.0 / full) + 1e-05)
        for b in range(N_SLAB):
            g_b = gain_ref[:, pl.ds(b * width, width)].astype(F32)
            nx[b, rs, :] = (xs[b] * inv * g_b).astype(BF16)
        gate = 1.0 / (1.0 + jnp.exp(-logit))
        cols[0, rs, :] = jnp.broadcast_to(mean, (step, 128))
        cols[1, rs, :] = jnp.broadcast_to(inv, (step, 128))
        cols[2, rs, :] = jnp.broadcast_to(gate, (step, 128))

    @pl.loop(0, ff // 256)
    def _(n):
        cs = pl.ds(pl.multiple_of(n * 256, 256), 256)
        acc = dot(nx[0], win[pl.ds(0, width), cs])
        for b in range(1, N_SLAB):
            acc += dot(nx[b], win[pl.ds(b * width, width), cs])
        pre[:, cs] = acc

    @pl.loop(0, rows // step)
    def _(i):
        rs = pl.ds(pl.multiple_of(i * step, step), step)
        p = pre[rs, :]
        gate = cols[2, rs, 0:1]
        sq = p * p
        tangent = jnp.tanh(ROOT * (p + 0.044715 * p * sq))
        half = 0.5 * (1.0 + tangent)
        act[rs, :] = p * half
        slp[rs, :] = gate * (
            half + 0.5 * p * (1.0 - tangent * tangent) * ROOT * (1.0 + 3.0 * 0.044715 * sq)
        )

    def back_from(b, first):
        base = pl.multiple_of(b * width, width)

        @pl.loop(0, ff // 256)
        def _(n):
            rs = pl.ds(pl.multiple_of(n * 256, 256), 256)
            value = dot_t(df[b], wout[rs, pl.ds(base, width)])
            if first:
                bk[:, rs] = value
            else:
                bk[:, rs] += value

    cp_wout.wait()
    back_from(slab, True)
    for tile in range(4):
        gather_copy(df, 1, tile, partner, 1, partner).wait_recv()
    back_from(partner, False)
    for tile in range(4):
        forward(df, 1, tile)
    back_from(far, False)
    for tile in range(4):
        gather_copy(df, 1, tile, far_partner, 2, partner).wait_recv()
    back_from(far_partner, False)

    @pl.loop(0, rows // step)
    def _(i):
        rs = pl.ds(pl.multiple_of(i * step, step), step)
        b = bk[rs, :]
        d = (b * slp[rs, :]).astype(BF16)
        delta[rs, :] = d
        d = d.astype(F32)
        g_sum = jnp.sum(act[rs, :] * b, axis=1, keepdims=True)
        one = jnp.sum(d * usum[0:1, :], axis=1, keepdims=True)
        two = jnp.sum(d * pre[rs, :], axis=1, keepdims=True)
        lane = iota((step, 128), 1)
        cols[3, rs, :] = jnp.where(lane == 0, g_sum, jnp.where(lane == 1, one, two))

    def grad_tile(b, tile):
        base = pl.multiple_of(b * width + tile * quarter, quarter)
        return dot_t(delta[...], win[pl.ds(base, quarter), :])

    def reduce_copy(kind, tile, src, dst, to):
        return pltpu.make_async_remote_copy(
            src_ref=src.at[tile],
            dst_ref=dst.at[tile],
            send_sem=rs_s.at[kind * 4 + tile],
            recv_sem=rs_r.at[kind * 4 + tile],
            device_id={"slab": to},
            device_id_type=MESH,
        )

    for tile in range(4):
        part_send[tile] = grad_tile(far_partner, tile).astype(BF16)
        reduce_copy(0, tile, part_send, part_recv, partner).start()
    for tile in range(4):
        far_acc[...] = grad_tile(far, tile)
        reduce_copy(0, tile, part_send, part_recv, partner).wait_recv()
        far_send[tile] = (far_acc[...] + part_recv[tile].astype(F32)).astype(BF16)
        reduce_copy(1, tile, far_send, far_recv, far).start()

    def stat_copy(n, to):
        return pltpu.make_async_remote_copy(
            src_ref=stat.at[0],
            dst_ref=stat.at[n],
            send_sem=st_s.at[n],
            recv_sem=st_r.at[n],
            device_id={"slab": to},
            device_id_type=MESH,
        )

    stat[0] = jnp.transpose(cols[3])[0:8]
    peers = ((1, partner), (2, far), (3, far_partner))
    for n, to in peers:
        stat_copy(n, to).start()
    for tile in range(4):
        mine_send[tile] = grad_tile(partner, tile).astype(BF16)
        reduce_copy(2, tile, mine_send, mine_recv, partner).start()
    for tile in range(4):
        own[tile] = grad_tile(slab, tile)
    for n, to in peers:
        stat_copy(n, to).wait_recv()
    sums = stat[0] + stat[1] + stat[2] + stat[3]
    sums = jnp.transpose(jnp.concatenate([sums] * 16, axis=0))
    gate = cols[2, :, 0:1]
    gate_grad = sums[:, 0:1] * gate * (1.0 - gate)
    mean_one = sums[:, 1:2] * (1.0 / full)
    mean_two = sums[:, 2:3] * (1.0 / full)
    mean = cols[0, :, 0:1]
    inv = cols[1, :, 0:1]
    for tile in range(4):
        cs = pl.ds(tile * quarter, quarter)
        glob = pl.ds(pl.multiple_of(slab * width + tile * quarter, quarter), quarter)
        x = xf[slab, :, cs].astype(F32)
        cgrad_ref[:, cs] = jnp.sum(x * gate_grad, axis=0, keepdims=True)
        reduce_copy(2, tile, mine_send, mine_recv, partner).wait_recv()
        total = own[tile] + mine_recv[tile].astype(F32)
        reduce_copy(1, tile, far_send, far_recv, far).wait_recv()
        total = total + far_recv[tile].astype(F32)
        scaled = total * gain_ref[:, glob].astype(F32)
        hat = (x - mean) * inv
        value = inv * (scaled - mean_one - hat * mean_two)
        value = value + gate_grad * cent_ref[:, glob].astype(F32)
        yy[:, cs] = value.astype(BF16)

    pack(pg, comp_t, yy)
    rg[mine, :] = pg[mine, :]
    send_all(pg, rg, 2)
    wait_bytes(rg, a2a_r.at[2])
    for tile in range(3):
        cs = pl.ds(tile * quarter, quarter)
        out_ref[:, cs] = dot(pick_t[0], rg[:, cs]).astype(BF16)
    value = dot(pick_t[1], rg[:, pl.ds(0, quarter)])
    value += dot(pick_t[2], rg[:, pl.ds(quarter, quarter)])
    value += dot(pick_t[3], rg[:, pl.ds(2 * quarter, quarter)])
    out_ref[:, pl.ds(3 * quarter, quarter)] = value.astype(BF16)

    wait_bytes(px, a2a_s.at[0])
    wait_bytes(pd, a2a_s.at[1])
    wait_bytes(pg, a2a_s.at[2])
    for tile in range(4):
        for which, buf in ((0, xf), (1, df)):
            gather_copy(buf, which, tile, slab, 0, far).wait_send()
            gather_copy(buf, which, tile, slab, 1, partner).wait_send()
            gather_copy(buf, which, tile, far, 2, partner).wait_send()
        reduce_copy(0, tile, part_send, part_recv, partner).wait_send()
        reduce_copy(1, tile, far_send, far_recv, far).wait_send()
        reduce_copy(2, tile, mine_send, mine_recv, partner).wait_send()
    for n, to in peers:
        stat_copy(n, to).wait_send()


def per_device(tokens, grad_out, position, centroid, gain, w_in, w_out):
    n_exp = lax.axis_size("expert")
    rows, width = tokens.shape
    full = centroid.shape[1]
    ff = w_in.shape[2]
    slots = n_exp * ROWS
    quarter = width // 4
    packed = 3 * quarter
    vmem = pl.BlockSpec(memory_space=pltpu.VMEM)
    hbm = pl.BlockSpec(memory_space=pl.ANY)
    buf = pltpu.VMEM
    dma = pltpu.SemaphoreType.DMA
    return pl.pallas_call(
        functools.partial(kernel, n_exp),
        out_shape=(
            jax.ShapeDtypeStruct((rows, width), BF16),
            jax.ShapeDtypeStruct((1, width), F32),
        ),
        in_specs=[vmem, vmem, vmem, hbm, hbm, hbm, hbm],
        out_specs=(vmem, vmem),
        scratch_shapes=[
            buf((rows, width), BF16),
            buf((rows, width), BF16),
            buf((full, ff), BF16),
            buf((ff, full), BF16),
            buf((4, slots, rows), BF16),
            buf((4, rows, slots), BF16),
            buf((slots, packed + 128), BF16),
            buf((slots, packed), BF16),
            buf((slots, packed + 128), BF16),
            buf((slots, packed), BF16),
            buf((4, rows, slots), BF16),
            buf((4, slots, rows), BF16),
            buf((N_SLAB, rows, width), BF16),
            buf((N_SLAB, rows, width), BF16),
            buf((N_SLAB, rows, width), BF16),
            buf((rows, ff), F32),
            buf((rows, ff), F32),
            buf((rows, ff), F32),
            buf((rows, ff), F32),
            buf((rows, ff), BF16),
            buf((8, ff), F32),
            buf((4, rows, 128), F32),
            buf((4, 8, rows), F32),
            buf((4, rows, quarter), BF16),
            buf((4, rows, quarter), BF16),
            buf((rows, quarter), F32),
            buf((4, rows, quarter), BF16),
            buf((4, rows, quarter), BF16),
            buf((4, rows, quarter), BF16),
            buf((4, rows, quarter), BF16),
            buf((4, rows, quarter), F32),
            buf((rows, width), BF16),
            buf((slots, packed), BF16),
            buf((slots, packed), BF16),
            dma((4,)),
            dma((3,)),
            dma((3,)),
            dma((24,)),
            dma((24,)),
            dma((12,)),
            dma((12,)),
            dma((4,)),
            dma((4,)),
        ],
        compiler_params=pltpu.CompilerParams(
            collective_id=0, has_side_effects=True, vmem_limit_bytes=56 * 2**20
        ),
        cost_estimate=pl.CostEstimate(
            flops=3 * 2 * rows * full * ff, bytes_accessed=4 * full * ff, transcendentals=rows * ff
        ),
    )(position.reshape(1, rows), centroid, gain, tokens, grad_out, w_in[0], w_out[0])


def solution(mesh):
    placed = (
        P("expert", "slab"),
        P("expert", "slab"),
        P("expert"),
        P("expert", None),
        P("expert", None),
        P("expert", None, "slab"),
        P("expert", "slab", None),
    )
    return jax.shard_map(
        per_device,
        mesh=mesh,
        in_specs=placed,
        out_specs=(P("expert", "slab"), P("expert", "slab")),
        check_vma=False,
    )
```

time: 337 us -> 95.5 us (0.28)
  waiting for transfers between devices: 186 us -> 0 us
  Pallas kernels: 0 us -> 91.1 us
  local copies, waits for them, and re-layouts: 52.5 us -> 3.13 us
  matrix products: 27.7 us -> 0 us
  other arithmetic: 26.5 us -> 0 us
  starting transfers between devices: 20.6 us -> 0 us
  between operations: 14 us -> 0.64 us
  blocking collectives: 7.27 us -> 0 us
    all_to_all x3 -> x0, waiting for transfers between devices: 98 us -> none  [the longest x1 57.6 us: per_device(): lax.all_to_all(pack(whole_x), 'expert', split_axis=0, concat_axis=0, tile...]
    pallas_call x0 -> x1, Pallas kernels: none -> 91.1 us  [per_device(): pl.pallas_call(functools.partial(kernel, n_exp), out_shape=(jax.ShapeDtyp...]
    reduce_scatter x1 -> x0, waiting for transfers between devices: 43.3 us -> none  [per_device(): lax.psum_scatter(lax.dot_general(weight_rows, delta, (((1,), (1,)), ((),...]
    all_gather x2 -> x0, waiting for transfers between devices: 43 us -> none  [the longest x1 25.5 us: per_device(): lax.all_gather(tokens, 'slab', axis=1, tiled=True)]
    dot_general x4 -> x0, matrix products: 27.7 us -> none  [the longest x1 11.2 us: per_device(): lax.dot_general(weight_rows, delta, (((1,), (1,)), ((), ())), preferred_e...]
    gather x3 -> x0, local copies, waits for them, and re-layouts: 21.4 us -> none  [the longest x2 20.2 us: pack(): jnp.take(rows, source, axis=0)]
    all_to_all x6 -> x0, local copies, waits for them, and re-layouts: 21.2 us -> none  [the longest x2 9.48 us: per_device(): lax.all_to_all(pack(whole_x), 'expert', split_axis=0, concat_axis=0, tile...]
    all_to_all x3 -> x0, starting transfers between devices: 20.4 us -> none  [the longest x1 7.16 us: per_device(): lax.all_to_all(pack(whole_x), 'expert', split_axis=0, concat_axis=0, tile...]
  transfers between devices with their start and end apart: 6 -> 0, of which waited for: 6 -> 0; matrix products, arithmetic and copies ran while one was open for 13% -> 0% of each run, Pallas kernels for 0% -> 0%
where the time goes in v1:
time: 95.5 us; the launch traced here: 94.9 us
  Pallas kernels  91.1 us (95%)
  local copies, waits for them, and re-layouts  3.13 us (3%)
    pallas_call x1, Pallas kernels, per_device(): pl.pallas_call(functools.partial(kernel, n_exp), out_shape=(jax.ShapeDtyp...  91.1 us
    unnamed x2, local copies, waits for them, and re-layouts  3.13 us

profile of v1, /device:TPU:1, one launch (start us, length us, event | category | flops | bytes accessed | tf_op | source)
XLA Modules:
  0.0 94.9 jit_solution(5971632286257639675)
XLA Ops:
  0.6 91.1 %shard_map.86 = (bf16[256,1024]{1,0:T(8,128)(2,1)}, f32[1,1024]{1,0:T(1,128)}) custom-call(s32[1,256]{1,0:T(1,128)} %bitcast.5, bf16[1,4096]{1,0:T(2,128)(2,1)} %cent_ref.1, bf16[1,4096]{1,0:T(2,128)(2,1)} %gain_ref.1, bf16[256,1024]{1,0:T(8,128)(2,1)} %tok_hbm.1, bf16[256,1024]{1,0:T(8,128)(2,1)} %dy_hbm.1, bf16[4096,1024]{1,0:T(8,128)(2,1)} %bitcast.3, ...), custom_call_target="tpu_custom_call" | custom-call | flops 6442450944 | bytes 16777216 | tf_op jit(solution)/shard_map/pallas_call | solution.py:436
  91.8 1.9 %copy.11 = bf16[256,1024]{1,0:T(8,128)(2,1)} copy(bf16[256,1024]{1,0:T(8,128)(2,1)} %get-tuple-element.4) | data formatting | bytes 1048576
  93.6 1.3 %copy.12 = f32[1,1024]{1,0:T(1,128)} copy(f32[1,1024]{1,0:T(1,128)} %get-tuple-element.5) | data formatting | bytes 8192

commit v2 on v1

v2 whole, which is shorter than its diff:
```python
import functools
import math

import jax
import jax.numpy as jnp
from jax import lax
from jax.experimental import pallas as pl
from jax.experimental.pallas import tpu as pltpu
from jax.sharding import PartitionSpec as P

F32 = jnp.float32
BF16 = jnp.bfloat16
MESH = pl.DeviceIdType.MESH
ROWS = 16
ROOT = math.sqrt(2.0 / math.pi)
N_SLAB = 4


def iota(shape, dim):
    return lax.broadcasted_iota(jnp.int32, shape, dim)


def onehot(mask):
    return jnp.where(mask, 1.0, 0.0).astype(BF16)


def dot(a, b):
    return jnp.dot(a, b, preferred_element_type=F32)


def dot_t(a, b):
    return lax.dot_general(a, b, (((1,), (1,)), ((), ())), preferred_element_type=F32)


def kernel(
    n_exp,
    pos_ref,
    cent_ref,
    gain_ref,
    tok_hbm,
    dy_hbm,
    win_hbm,
    wout_hbm,
    out_ref,
    cgrad_ref,
    tok,
    gdy,
    win,
    wout,
    pick,
    pick_t,
    px0,
    px1,
    pd0,
    pd1,
    rx0,
    rx1,
    rd0,
    rd1,
    comp,
    comp_t,
    xf,
    df,
    nx,
    pre,
    act,
    slp,
    bk,
    delta,
    usum,
    cols,
    stat,
    part_send,
    part_recv,
    far_send,
    far_recv,
    mine_send,
    mine_recv,
    own,
    yy,
    pg0,
    pg1,
    rg0,
    rg1,
    lsem,
    a2a_s,
    a2a_r,
    ag_s,
    ag_r,
    rs_s,
    rs_r,
    st_s,
    st_r,
):
    rows, width = tok.shape
    full = N_SLAB * width
    ff = win.shape[1]
    half = width // 2
    q = half // 4
    tile_w = width // 4
    half_rows = rows // 2
    slots = n_exp * ROWS
    me = lax.axis_index("expert")
    slab = lax.axis_index("slab")
    hi, core = slab // 2, slab % 2
    partner = hi * 2 + (1 - core)
    far = (1 - hi) * 2 + core
    far_partner = (1 - hi) * 2 + (1 - core)

    cp_tok = pltpu.make_async_copy(tok_hbm, tok, lsem.at[0])
    cp_dy = pltpu.make_async_copy(dy_hbm, gdy, lsem.at[1])
    cp_win = pltpu.make_async_copy(win_hbm, win, lsem.at[2])
    cp_wout = pltpu.make_async_copy(wout_hbm, wout, lsem.at[3])
    cp_tok.start()
    cp_dy.start()

    bar = pltpu.get_barrier_semaphore()

    @pl.loop(1, n_exp)
    def _(k):
        pl.semaphore_signal(
            bar, inc=1, device_id={"expert": lax.rem(me + k, n_exp)}, device_id_type=MESH
        )

    for peer in (partner, far, far_partner):
        pl.semaphore_signal(bar, inc=1, device_id={"slab": peer}, device_id_type=MESH)
    cp_win.start()
    cp_wout.start()

    pos = pos_ref[...]
    tgt = lax.div(pos, rows)
    row = pos - tgt * rows
    hit = iota((n_exp, rows), 0) == tgt
    before = dot(onehot(hit), onehot(iota((rows, rows), 0) < iota((rows, rows), 1)))
    rank = jnp.sum(jnp.where(hit, before, 0.0), axis=0, keepdims=True).astype(jnp.int32)
    third = lax.shift_right_logical(rank * 11, 5)
    rem3 = rank - 3 * third
    slot = [tgt * ROWS + rank]
    for j in range(3):
        slot.append(jnp.where(rem3 == j, tgt * ROWS + 12 + third, -1))
    for k in range(4):
        pick[k] = onehot(iota((slots, rows), 0) == slot[k])

    row_one = jnp.broadcast_to((row + 1).astype(F32), (128, rows))
    meta = None
    for k in range(4):
        marks = jnp.where(iota((128, rows), 0) // 32 == k, row_one, 0.0).astype(BF16)
        term = dot_t(pick[k], marks)
        meta = term if meta is None else meta + term
    px0[:, pl.ds(3 * q, 128)] = meta.astype(BF16)

    mine = pl.ds(pl.multiple_of(me * ROWS, ROWS), ROWS)

    def pack(into, keep, take, source, c):
        last = source[:, pl.ds(c * half + 3 * q, q)]
        for j in range(3):
            cs = pl.ds(j * q, q)
            value = dot(take[0], source[:, pl.ds(c * half + j * q, q)]) + dot(take[1 + j], last)
            into[:, cs] = value.astype(BF16)
        keep[mine, :] = into[mine, :]

    def unpack(into, lead, take, source, c):
        into[lead + (slice(None), pl.ds(c * half, 3 * q))] = dot(
            take[0], source[:, pl.ds(0, 3 * q)]
        ).astype(BF16)
        value = dot(take[1], source[:, pl.ds(0, q)])
        value += dot(take[2], source[:, pl.ds(q, q)])
        value += dot(take[3], source[:, pl.ds(2 * q, q)])
        into[lead + (slice(None), pl.ds(c * half + 3 * q, q))] = value.astype(BF16)

    def send_all(source, target, idx):
        @pl.loop(1, n_exp)
        def _(k):
            d = lax.rem(me + k, n_exp)
            pltpu.make_async_remote_copy(
                src_ref=source.at[pl.ds(pl.multiple_of(d * ROWS, ROWS), ROWS)],
                dst_ref=target.at[mine],
                send_sem=a2a_s.at[idx],
                recv_sem=a2a_r.at[idx],
                device_id={"expert": d},
                device_id_type=MESH,
            ).start()

    def wait_bytes(ref, sem):
        part = ref.at[pl.ds(0, (n_exp - 1) * ROWS)]
        pltpu.make_async_copy(part, part, sem).wait()

    cp_tok.wait()
    pack(px0, rx0, pick, tok, 0)
    pl.semaphore_wait(bar, n_exp - 1 + 3)
    send_all(px0, rx0, 0)
    pack(px1, rx1, pick, tok, 1)
    send_all(px1, rx1, 1)
    cp_dy.wait()
    pack(pd0, rd0, pick, gdy, 0)
    pack(pd1, rd1, pick, gdy, 1)

    for k in range(4):
        turned = jnp.transpose(jnp.broadcast_to(slot[k].astype(F32), (128, rows)))[:, 0:1]
        pick_t[k] = onehot(iota((rows, slots), 1).astype(F32) == turned)
    cp_win.wait()
    gain_rows = jnp.broadcast_to(gain_ref[...], (16, full))

    @pl.loop(0, ff // 256)
    def _(n):
        cs = pl.ds(pl.multiple_of(n * 256, 256), 256)
        usum[:, cs] = dot(gain_rows, win[:, cs])[0:8]

    def gather_copy(buf, idx, rs, c, source, kind, to):
        block = buf.at[source, rs, pl.ds(c * half, half)]
        return pltpu.make_async_remote_copy(
            src_ref=block,
            dst_ref=block,
            send_sem=ag_s.at[idx * 3 + kind],
            recv_sem=ag_r.at[idx * 3 + kind],
            device_id={"slab": to},
            device_id_type=MESH,
        )

    every = pl.ds(0, rows)

    def x_copy(c, source, kind, to):
        return gather_copy(xf, c, every, c, source, kind, to)

    def d_copy(h, c, source, kind, to):
        return gather_copy(
            df, 2 + 2 * h + c, pl.ds(h * half_rows, half_rows), c, source, kind, to
        )

    def x_dense(recv, c):
        unpack(xf, (slab,), comp, recv, c)
        x_copy(c, slab, 0, far).start()
        x_copy(c, slab, 1, partner).start()

    def d_start(h, c):
        d_copy(h, c, slab, 0, far).start()
        d_copy(h, c, slab, 1, partner).start()

    wait_bytes(rx0, a2a_r.at[0])
    marks_in = rx0[:, pl.ds(3 * q, 128)].astype(F32)
    marks_t = jnp.transpose(marks_in)
    for k in range(4):
        comp[k] = onehot((iota((rows, slots), 0) + 1).astype(F32) == marks_t[32 * k : 32 * k + 1])
    x_dense(rx0, 0)
    send_all(pd0, rd0, 2)
    wait_bytes(rx1, a2a_r.at[1])
    x_dense(rx1, 1)
    send_all(pd1, rd1, 3)
    for k in range(4):
        comp_t[k] = onehot(
            (iota((slots, rows), 1) + 1).astype(F32) == marks_in[:, 32 * k : 32 * k + 1]
        )
    x_copy(0, far, 0, far).wait_recv()
    x_copy(0, far, 2, partner).start()
    wait_bytes(rd0, a2a_r.at[2])
    unpack(df, (slab,), comp, rd0, 0)
    d_start(0, 0)
    x_copy(1, far, 0, far).wait_recv()
    x_copy(1, far, 2, partner).start()
    for c in range(2):
        x_copy(c, partner, 1, partner).wait_recv()
    for c in range(2):
        x_copy(c, far_partner, 2, partner).wait_recv()

    step = 16

    @pl.loop(0, rows // step)
    def _(i):
        rs = pl.ds(pl.multiple_of(i * step, step), step)
        xs = [xf[b, rs, :].astype(F32) for b in range(N_SLAB)]
        total = None
        logit = None
        for b in range(N_SLAB):
            c_b = cent_ref[:, pl.ds(b * width, width)].astype(F32)
            t_b = jnp.sum(xs[b], axis=1, keepdims=True)
            l_b = jnp.sum(xs[b] * c_b, axis=1, keepdims=True)
            total = t_b if total is None else total + t_b
            logit = l_b if logit is None else logit + l_b
        mean = total * (1.0 / full)
        spread = None
        for b in range(N_SLAB):
            xs[b] = xs[b] - mean
            v_b = jnp.sum(xs[b] * xs[b], axis=1, keepdims=True)
            spread = v_b if spread is None else spread + v_b
        inv = lax.rsqrt(spread * (1.0 / full) + 1e-05)
        for b in range(N_SLAB):
            g_b = gain_ref[:, pl.ds(b * width, width)].astype(F32)
            nx[b, rs, :] = (xs[b] * inv * g_b).astype(BF16)
        gate = 1.0 / (1.0 + jnp.exp(-logit))
        cols[0, rs, :] = jnp.broadcast_to(mean, (step, 128))
        cols[1, rs, :] = jnp.broadcast_to(inv, (step, 128))
        cols[2, rs, :] = jnp.broadcast_to(gate, (step, 128))
    wait_bytes(rd1, a2a_r.at[3])
    unpack(df, (slab,), comp, rd1, 1)
    d_start(0, 1)
    d_start(1, 0)
    d_start(1, 1)

    for n in range(ff // 256):
        cs = pl.ds(n * 256, 256)
        acc = dot(nx[0], win[pl.ds(0, width), cs])
        for b in range(1, N_SLAB):
            acc += dot(nx[b], win[pl.ds(b * width, width), cs])
        pre[:, cs] = acc

    @pl.loop(0, rows // step, unroll=2)
    def _(i):
        rs = pl.ds(pl.multiple_of(i * step, step), step)
        p = pre[rs, :]
        gate = cols[2, rs, 0:1]
        sq = p * p
        tangent = jnp.tanh(ROOT * (p + 0.044715 * p * sq))
        mid = 0.5 * (1.0 + tangent)
        act[rs, :] = p * mid
        slp[rs, :] = gate * (
            mid + 0.5 * p * (1.0 - tangent * tangent) * ROOT * (1.0 + 3.0 * 0.044715 * sq)
        )

    cp_wout.wait()

    def back_from(h, sources, first):
        hs = pl.ds(h * half_rows, half_rows)

        for n in range(ff // 256):
            rs = pl.ds(n * 256, 256)
            value = None
            for b in sources:
                base = pl.multiple_of(b * width, width)
                term = dot_t(df[b, hs, :], wout[rs, pl.ds(base, width)])
                value = term if value is None else value + term
            if first:
                bk[hs, rs] = value
            else:
                bk[hs, rs] += value

    def grad_tile(b, tile, rs):
        base = pl.multiple_of(b * width + tile * tile_w, tile_w)
        return dot_t(delta[rs, :], win[pl.ds(base, tile_w), :])

    def reduce_copy(kind, n, src, dst, to):
        return pltpu.make_async_remote_copy(
            src_ref=src.at[n],
            dst_ref=dst.at[n],
            send_sem=rs_s.at[kind * 8 + n],
            recv_sem=rs_r.at[kind * 8 + n],
            device_id={"slab": to},
            device_id_type=MESH,
        )

    def part_copy(n):
        return reduce_copy(0, n, part_send, part_recv, partner)

    def far_copy(n):
        return reduce_copy(1, n, far_send, far_recv, far)

    def mine_copy(n):
        return reduce_copy(2, n, mine_send, mine_recv, partner)

    for h in range(2):
        hs = pl.ds(h * half_rows, half_rows)
        for c in range(2):
            d_copy(h, c, partner, 1, partner).wait_recv()
        back_from(h, (slab, partner), True)
        for c in range(2):
            d_copy(h, c, far, 0, far).wait_recv()
            d_copy(h, c, far, 2, partner).start()
        back_from(h, (far,), False)
        for c in range(2):
            d_copy(h, c, far_partner, 2, partner).wait_recv()
        back_from(h, (far_partner,), False)

        @pl.loop(0, half_rows // step, unroll=4)
        def _(i):
            rs = pl.ds(pl.multiple_of(h * half_rows + i * step, step), step)
            b = bk[rs, :]
            d = (b * slp[rs, :]).astype(BF16)
            delta[rs, :] = d
            d = d.astype(F32)
            g_sum = jnp.sum(act[rs, :] * b, axis=1, keepdims=True)
            one = jnp.sum(d * usum[0:1, :], axis=1, keepdims=True)
            two = jnp.sum(d * pre[rs, :], axis=1, keepdims=True)
            lane = iota((step, 128), 1)
            cols[3, rs, :] = jnp.where(lane == 0, g_sum, jnp.where(lane == 1, one, two))

        for tile in range(4):
            part_send[h * 4 + tile] = grad_tile(far_partner, tile, hs).astype(BF16)
            part_copy(h * 4 + tile).start()
        for tile in range(4):
            value = grad_tile(far, tile, hs)
            part_copy(h * 4 + tile).wait_recv()
            far_send[h * 4 + tile] = (value + part_recv[h * 4 + tile].astype(F32)).astype(BF16)
            far_copy(h * 4 + tile).start()
    def stat_copy(n, to):
        return pltpu.make_async_remote_copy(
            src_ref=stat.at[0],
            dst_ref=stat.at[n],
            send_sem=st_s.at[n],
            recv_sem=st_r.at[n],
            device_id={"slab": to},
            device_id_type=MESH,
        )

    stat[0] = jnp.transpose(cols[3])[0:8]
    peers = ((1, partner), (2, far), (3, far_partner))
    for n, to in peers:
        stat_copy(n, to).start()
    for tile in range(4):
        mine_send[tile] = grad_tile(partner, tile, every).astype(BF16)
        mine_copy(tile).start()
    for tile in range(4):
        own[tile] = grad_tile(slab, tile, every)
    for n, to in peers:
        stat_copy(n, to).wait_recv()
    sums = stat[0] + stat[1] + stat[2] + stat[3]
    sums = jnp.transpose(jnp.concatenate([sums] * 16, axis=0))
    gate = cols[2, :, 0:1]
    gate_grad = sums[:, 0:1] * gate * (1.0 - gate)
    mean_one = sums[:, 1:2] * (1.0 / full)
    mean_two = sums[:, 2:3] * (1.0 / full)
    mean = cols[0, :, 0:1]
    inv = cols[1, :, 0:1]

    for tile in range(4):
        cs = pl.ds(tile * tile_w, tile_w)
        x = xf[slab, :, cs].astype(F32)
        cgrad_ref[:, cs] = jnp.sum(x * gate_grad, axis=0, keepdims=True)
        mine_copy(tile).wait_recv()
        own[tile] += mine_recv[tile].astype(F32)
    for tile in range(4):
        cs = pl.ds(tile * tile_w, tile_w)
        glob = pl.ds(pl.multiple_of(slab * width + tile * tile_w, tile_w), tile_w)
        gain_part = gain_ref[:, glob].astype(F32)
        cent_part = cent_ref[:, glob].astype(F32)
        for h in range(2):
            lo, up = h * half_rows, (h + 1) * half_rows
            hs = pl.ds(lo, half_rows)
            x = xf[slab, hs, cs].astype(F32)
            far_copy(h * 4 + tile).wait_recv()
            total = own[tile, hs, :] + far_recv[h * 4 + tile].astype(F32)
            scaled = total * gain_part
            hat = (x - mean[lo:up]) * inv[lo:up]
            value = inv[lo:up] * (scaled - mean_one[lo:up] - hat * mean_two[lo:up])
            value = value + gate_grad[lo:up] * cent_part
            yy[hs, cs] = value.astype(BF16)
        if tile == 1:
            pack(pg0, rg0, comp_t, yy, 0)
            send_all(pg0, rg0, 4)
    pack(pg1, rg1, comp_t, yy, 1)
    send_all(pg1, rg1, 5)
    wait_bytes(rg0, a2a_r.at[4])
    unpack(out_ref, (), pick_t, rg0, 0)
    wait_bytes(rg1, a2a_r.at[5])
    unpack(out_ref, (), pick_t, rg1, 1)

    for idx, buf in enumerate((px0, px1, pd0, pd1, pg0, pg1)):
        wait_bytes(buf, a2a_s.at[idx])
    for c in range(2):
        x_copy(c, slab, 0, far).wait_send()
        x_copy(c, slab, 1, partner).wait_send()
        x_copy(c, far, 2, partner).wait_send()
        for h in range(2):
            d_copy(h, c, slab, 0, far).wait_send()
            d_copy(h, c, slab, 1, partner).wait_send()
            d_copy(h, c, far, 2, partner).wait_send()
    for n in range(8):
        part_copy(n).wait_send()
        far_copy(n).wait_send()
    for n in range(4):
        mine_copy(n).wait_send()
    for n, to in peers:
        stat_copy(n, to).wait_send()


def hand_on(out_in, cgrad_in, out_ref, cgrad_ref):
    out_ref[...] = out_in[...]
    cgrad_ref[...] = cgrad_in[...]


def per_device(tokens, grad_out, position, centroid, gain, w_in, w_out):
    n_exp = lax.axis_size("expert")
    rows, width = tokens.shape
    full = centroid.shape[1]
    ff = w_in.shape[2]
    slots = n_exp * ROWS
    packed = 3 * width // 8
    vmem = pl.BlockSpec(memory_space=pltpu.VMEM)
    hbm = pl.BlockSpec(memory_space=pl.ANY)
    buf = pltpu.VMEM
    dma = pltpu.SemaphoreType.DMA
    shapes = (
        jax.ShapeDtypeStruct((rows, width), BF16),
        jax.ShapeDtypeStruct((1, width), F32),
    )
    out, cgrad = pl.pallas_call(
        functools.partial(kernel, n_exp),
        out_shape=shapes,
        in_specs=[vmem, vmem, vmem, hbm, hbm, hbm, hbm],
        out_specs=(vmem, vmem),
        scratch_shapes=[
            buf((rows, width), BF16),
            buf((rows, width), BF16),
            buf((full, ff), BF16),
            buf((ff, full), BF16),
            buf((4, slots, rows), BF16),
            buf((4, rows, slots), BF16),
            buf((slots, packed + 128), BF16),
            buf((slots, packed), BF16),
            buf((slots, packed), BF16),
            buf((slots, packed), BF16),
            buf((slots, packed + 128), BF16),
            buf((slots, packed), BF16),
            buf((slots, packed), BF16),
            buf((slots, packed), BF16),
            buf((4, rows, slots), BF16),
            buf((4, slots, rows), BF16),
            buf((N_SLAB, rows, width), BF16),
            buf((N_SLAB, rows, width), BF16),
            buf((N_SLAB, rows, width), BF16),
            buf((rows, ff), F32),
            buf((rows, ff), F32),
            buf((rows, ff), F32),
            buf((rows, ff), F32),
            buf((rows, ff), BF16),
            buf((8, ff), F32),
            buf((4, rows, 128), F32),
            buf((4, 8, rows), F32),
            buf((8, rows // 2, width // 4), BF16),
            buf((8, rows // 2, width // 4), BF16),
            buf((8, rows // 2, width // 4), BF16),
            buf((8, rows // 2, width // 4), BF16),
            buf((4, rows, width // 4), BF16),
            buf((4, rows, width // 4), BF16),
            buf((4, rows, width // 4), F32),
            buf((rows, width), BF16),
            buf((slots, packed), BF16),
            buf((slots, packed), BF16),
            buf((slots, packed), BF16),
            buf((slots, packed), BF16),
            dma((4,)),
            dma((6,)),
            dma((6,)),
            dma((18,)),
            dma((18,)),
            dma((20,)),
            dma((20,)),
            dma((4,)),
            dma((4,)),
        ],
        compiler_params=pltpu.CompilerParams(
            collective_id=0, has_side_effects=True, vmem_limit_bytes=56 * 2**20
        ),
        cost_estimate=pl.CostEstimate(
            flops=3 * 2 * rows * full * ff, bytes_accessed=4 * full * ff, transcendentals=rows * ff
        ),
    )(position.reshape(1, rows), centroid, gain, tokens, grad_out, w_in[0], w_out[0])
    return pl.pallas_call(
        hand_on,
        out_shape=shapes,
        in_specs=[vmem, vmem],
        out_specs=(vmem, vmem),
    )(out, cgrad)


def solution(mesh):
    placed = (
        P("expert", "slab"),
        P("expert", "slab"),
        P("expert"),
        P("expert", None),
        P("expert", None),
        P("expert", None, "slab"),
        P("expert", "slab", None),
    )
    return jax.shard_map(
        per_device,
        mesh=mesh,
        in_specs=placed,
        out_specs=(P("expert", "slab"), P("expert", "slab")),
        check_vma=False,
    )
```

time: 95.5 us -> 92.5 us (0.969)
  local copies, waits for them, and re-layouts: 3.13 us -> 0 us
    unnamed x2 -> x0, local copies, waits for them, and re-layouts: 3.13 us -> none
    pallas_call x1 -> x2, Pallas kernels: 91.1 us -> 91.6 us  [the longest x1 89.8 us: per_device(): pl.pallas_call(functools.partial(kernel, n_exp), out_shape=shapes, in_spe...]
where the time goes in v2:
time: 92.5 us; the launch traced here: 92.3 us
  Pallas kernels  91.6 us (99%)
    pallas_call x1, Pallas kernels, per_device(): pl.pallas_call(functools.partial(kernel, n_exp), out_shape=shapes, in_spe...  89.8 us
    pallas_call x1, Pallas kernels, per_device(): pl.pallas_call(hand_on, out_shape=shapes, in_specs=[vmem, vmem], out_spec...  1.87 us

profile of v2, /device:TPU:1, one launch (start us, length us, event | category | flops | bytes accessed | tf_op | source)
XLA Modules:
  0.0 92.3 jit_solution(9946409940945446998)
XLA Ops:
  0.6 89.8 %shard_map.86 = (bf16[256,1024]{1,0:T(8,128)(2,1)}, f32[1,1024]{1,0:T(1,128)}) custom-call(s32[1,256]{1,0:T(1,128)} %bitcast.5, bf16[1,4096]{1,0:T(2,128)(2,1)} %cent_ref.1, bf16[1,4096]{1,0:T(2,128)(2,1)} %gain_ref.1, bf16[256,1024]{1,0:T(8,128)(2,1)} %tok_hbm.1, bf16[256,1024]{1,0:T(8,128)(2,1)} %dy_hbm.1, bf16[4096,1024]{1,0:T(8,128)(2,1)} %bitcast.3, ...), custom_call_target="tpu_custom_call" | custom-call | flops 6442450944 | bytes 16777216 | tf_op jit(solution)/shard_map/pallas_call | solution.py:494
  90.4 1.9 %shard_map.87 = (bf16[256,1024]{1,0:T(8,128)(2,1)}, f32[1,1024]{1,0:T(1,128)}) custom-call(bf16[256,1024]{1,0:T(8,128)(2,1)} %get-tuple-element.4.out_in, f32[1,1024]{1,0:T(1,128)} %get-tuple-element.5.cgrad_in), custom_call_target="tpu_custom_call" | custom-call | tf_op jit(solution)/shard_map/pallas_call | solution.py:556

commit v3 on v2

--- a/solution.py
+++ b/solution.py
@@ -257,6 +257,11 @@
     d_start(0, 0)
     x_copy(1, far, 0, far).wait_recv()
     x_copy(1, far, 2, partner).start()
+    wait_bytes(rd1, a2a_r.at[3])
+    unpack(df, (slab,), comp, rd1, 1)
+    d_start(0, 1)
+    d_start(1, 0)
+    d_start(1, 1)
     for c in range(2):
         x_copy(c, partner, 1, partner).wait_recv()
     for c in range(2):
@@ -264,7 +269,7 @@
 
     step = 16
 
-    @pl.loop(0, rows // step)
+    @pl.loop(0, rows // step, unroll=2)
     def _(i):
         rs = pl.ds(pl.multiple_of(i * step, step), step)
         xs = [xf[b, rs, :].astype(F32) for b in range(N_SLAB)]
@@ -290,12 +295,6 @@
         cols[0, rs, :] = jnp.broadcast_to(mean, (step, 128))
         cols[1, rs, :] = jnp.broadcast_to(inv, (step, 128))
         cols[2, rs, :] = jnp.broadcast_to(gate, (step, 128))
-    wait_bytes(rd1, a2a_r.at[3])
-    unpack(df, (slab,), comp, rd1, 1)
-    d_start(0, 1)
-    d_start(1, 0)
-    d_start(1, 1)
-
     for n in range(ff // 256):
         cs = pl.ds(n * 256, 256)
         acc = dot(nx[0], win[pl.ds(0, width), cs])
@@ -356,19 +355,16 @@
     def mine_copy(n):
         return reduce_copy(2, n, mine_send, mine_recv, partner)
 
-    for h in range(2):
-        hs = pl.ds(h * half_rows, half_rows)
-        for c in range(2):
-            d_copy(h, c, partner, 1, partner).wait_recv()
-        back_from(h, (slab, partner), True)
+    def forward(h):
         for c in range(2):
             d_copy(h, c, far, 0, far).wait_recv()
             d_copy(h, c, far, 2, partner).start()
-        back_from(h, (far,), False)
+
+    def arrived(h, source, kind):
         for c in range(2):
-            d_copy(h, c, far_partner, 2, partner).wait_recv()
-        back_from(h, (far_partner,), False)
-
+            d_copy(h, c, source, kind, partner).wait_recv()
+
+    def delta_of(h):
         @pl.loop(0, half_rows // step, unroll=4)
         def _(i):
             rs = pl.ds(pl.multiple_of(h * half_rows + i * step, step), step)
@@ -382,14 +378,20 @@
             lane = iota((step, 128), 1)
             cols[3, rs, :] = jnp.where(lane == 0, g_sum, jnp.where(lane == 1, one, two))
 
+    def parts(h):
+        hs = pl.ds(h * half_rows, half_rows)
         for tile in range(4):
             part_send[h * 4 + tile] = grad_tile(far_partner, tile, hs).astype(BF16)
             part_copy(h * 4 + tile).start()
+
+    def fars(h):
+        hs = pl.ds(h * half_rows, half_rows)
         for tile in range(4):
             value = grad_tile(far, tile, hs)
             part_copy(h * 4 + tile).wait_recv()
             far_send[h * 4 + tile] = (value + part_recv[h * 4 + tile].astype(F32)).astype(BF16)
             far_copy(h * 4 + tile).start()
+
     def stat_copy(n, to):
         return pltpu.make_async_remote_copy(
             src_ref=stat.at[0],
@@ -400,6 +402,22 @@
             device_id_type=MESH,
         )
 
+    arrived(0, partner, 1)
+    back_from(0, (slab, partner), True)
+    forward(0)
+    back_from(0, (far,), False)
+    arrived(0, far_partner, 2)
+    back_from(0, (far_partner,), False)
+    delta_of(0)
+    parts(0)
+    arrived(1, partner, 1)
+    forward(1)
+    back_from(1, (slab, partner, far), True)
+    fars(0)
+    arrived(1, far_partner, 2)
+    back_from(1, (far_partner,), False)
+    delta_of(1)
+    parts(1)
     stat[0] = jnp.transpose(cols[3])[0:8]
     peers = ((1, partner), (2, far), (3, far_partner))
     for n, to in peers:
@@ -407,6 +425,7 @@
     for tile in range(4):
         mine_send[tile] = grad_tile(partner, tile, every).astype(BF16)
         mine_copy(tile).start()
+    fars(1)
     for tile in range(4):
         own[tile] = grad_tile(slab, tile, every)
     for n, to in peers:

time: 92.5 us -> 84.7 us (0.916)
  Pallas kernels: 91.6 us -> 83.8 us
    pallas_call x1, Pallas kernels: 89.8 us -> 81.9 us  [per_device(): pl.pallas_call(functools.partial(kernel, n_exp), out_shape=shapes, in_spe...]
where the time goes in v3:
time: 84.7 us; the launch traced here: 84.5 us
  Pallas kernels  83.8 us (99%)
    pallas_call x1, Pallas kernels, per_device(): pl.pallas_call(functools.partial(kernel, n_exp), out_shape=shapes, in_spe...  81.9 us
    pallas_call x1, Pallas kernels, per_device(): pl.pallas_call(hand_on, out_shape=shapes, in_specs=[vmem, vmem], out_spec...  1.87 us

profile of v3, /device:TPU:1, one launch (start us, length us, event | category | flops | bytes accessed | tf_op | source)
XLA Modules:
  0.0 84.5 jit_solution(5719464416826408197)
XLA Ops:
  0.6 81.9 %shard_map.86 = (bf16[256,1024]{1,0:T(8,128)(2,1)}, f32[1,1024]{1,0:T(1,128)}) custom-call(s32[1,256]{1,0:T(1,128)} %bitcast.5, bf16[1,4096]{1,0:T(2,128)(2,1)} %cent_ref.1, bf16[1,4096]{1,0:T(2,128)(2,1)} %gain_ref.1, bf16[256,1024]{1,0:T(8,128)(2,1)} %tok_hbm.1, bf16[256,1024]{1,0:T(8,128)(2,1)} %dy_hbm.1, bf16[4096,1024]{1,0:T(8,128)(2,1)} %bitcast.3, ...), custom_call_target="tpu_custom_call" | custom-call | flops 6442450944 | bytes 16777216 | tf_op jit(solution)/shard_map/pallas_call | solution.py:513
  82.6 1.9 %shard_map.87 = (bf16[256,1024]{1,0:T(8,128)(2,1)}, f32[1,1024]{1,0:T(1,128)}) custom-call(bf16[256,1024]{1,0:T(8,128)(2,1)} %get-tuple-element.4.out_in, f32[1,1024]{1,0:T(1,128)} %get-tuple-element.5.cgrad_in), custom_call_target="tpu_custom_call" | custom-call | tf_op jit(solution)/shard_map/pallas_call | solution.py:575

commit v4 on v3

--- a/solution.py
+++ b/solution.py
@@ -422,10 +422,10 @@
     peers = ((1, partner), (2, far), (3, far_partner))
     for n, to in peers:
         stat_copy(n, to).start()
+    fars(1)
     for tile in range(4):
         mine_send[tile] = grad_tile(partner, tile, every).astype(BF16)
         mine_copy(tile).start()
-    fars(1)
     for tile in range(4):
         own[tile] = grad_tile(slab, tile, every)
     for n, to in peers:

time: 84.7 us -> 83.9 us (level)
  no operation moved by 1% of the time
where the time goes in v4:
time: 83.9 us; the launch traced here: 83.7 us
  Pallas kernels  83 us (99%)
    pallas_call x1, Pallas kernels, per_device(): pl.pallas_call(functools.partial(kernel, n_exp), out_shape=shapes, in_spe...  81.1 us
    pallas_call x1, Pallas kernels, per_device(): pl.pallas_call(hand_on, out_shape=shapes, in_specs=[vmem, vmem], out_spec...  1.87 us

profile of v4, /device:TPU:1, one launch (start us, length us, event | category | flops | bytes accessed | tf_op | source)
XLA Modules:
  0.0 83.7 jit_solution(6856020519249199565)
XLA Ops:
  0.6 81.1 %shard_map.86 = (bf16[256,1024]{1,0:T(8,128)(2,1)}, f32[1,1024]{1,0:T(1,128)}) custom-call(s32[1,256]{1,0:T(1,128)} %bitcast.5, bf16[1,4096]{1,0:T(2,128)(2,1)} %cent_ref.1, bf16[1,4096]{1,0:T(2,128)(2,1)} %gain_ref.1, bf16[256,1024]{1,0:T(8,128)(2,1)} %tok_hbm.1, bf16[256,1024]{1,0:T(8,128)(2,1)} %dy_hbm.1, bf16[4096,1024]{1,0:T(8,128)(2,1)} %bitcast.3, ...), custom_call_target="tpu_custom_call" | custom-call | flops 6442450944 | bytes 16777216 | tf_op jit(solution)/shard_map/pallas_call | solution.py:513
  81.8 1.9 %shard_map.87 = (bf16[256,1024]{1,0:T(8,128)(2,1)}, f32[1,1024]{1,0:T(1,128)}) custom-call(bf16[256,1024]{1,0:T(8,128)(2,1)} %get-tuple-element.4.out_in, f32[1,1024]{1,0:T(1,128)} %get-tuple-element.5.cgrad_in), custom_call_target="tpu_custom_call" | custom-call | tf_op jit(solution)/shard_map/pallas_call | solution.py:575

commit v5 on v4

--- a/solution.py
+++ b/solution.py
@@ -412,8 +412,9 @@
     parts(0)
     arrived(1, partner, 1)
     forward(1)
-    back_from(1, (slab, partner, far), True)
+    back_from(1, (slab, partner), True)
     fars(0)
+    back_from(1, (far,), False)
     arrived(1, far_partner, 2)
     back_from(1, (far_partner,), False)
     delta_of(1)

time: 83.9 us -> 84.4 us (level)
  no operation moved by 1% of the time
where the time goes in v5:
time: 84.4 us; the launch traced here: 84.2 us
  Pallas kernels  83.5 us (99%)
    pallas_call x1, Pallas kernels, per_device(): pl.pallas_call(functools.partial(kernel, n_exp), out_shape=shapes, in_spe...  81.6 us
    pallas_call x1, Pallas kernels, per_device(): pl.pallas_call(hand_on, out_shape=shapes, in_specs=[vmem, vmem], out_spec...  1.87 us

profile of v5, /device:TPU:1, one launch (start us, length us, event | category | flops | bytes accessed | tf_op | source)
XLA Modules:
  0.0 84.2 jit_solution(1531446486423005486)
XLA Ops:
  0.6 81.6 %shard_map.86 = (bf16[256,1024]{1,0:T(8,128)(2,1)}, f32[1,1024]{1,0:T(1,128)}) custom-call(s32[1,256]{1,0:T(1,128)} %bitcast.5, bf16[1,4096]{1,0:T(2,128)(2,1)} %cent_ref.1, bf16[1,4096]{1,0:T(2,128)(2,1)} %gain_ref.1, bf16[256,1024]{1,0:T(8,128)(2,1)} %tok_hbm.1, bf16[256,1024]{1,0:T(8,128)(2,1)} %dy_hbm.1, bf16[4096,1024]{1,0:T(8,128)(2,1)} %bitcast.3, ...), custom_call_target="tpu_custom_call" | custom-call | flops 6442450944 | bytes 16777216 | tf_op jit(solution)/shard_map/pallas_call | solution.py:514
  82.3 1.9 %shard_map.87 = (bf16[256,1024]{1,0:T(8,128)(2,1)}, f32[1,1024]{1,0:T(1,128)}) custom-call(bf16[256,1024]{1,0:T(8,128)(2,1)} %get-tuple-element.4.out_in, f32[1,1024]{1,0:T(1,128)} %get-tuple-element.5.cgrad_in), custom_call_target="tpu_custom_call" | custom-call | tf_op jit(solution)/shard_map/pallas_call | solution.py:576
